TPU v7x, 32 devices: a whole 2x2x4 slice. The times are simulated.
32 devices in a mesh: seq: 8 (over z, core), chan: 4 (over y, x).
Axes of the slice: x: 2, y: 2, z: 4, core: 2. Of those that a mesh axis runs over, the one named last changes fastest.
Arguments:
- layer_source: bfloat16 [8192, 4096], P('seq', 'chan'), may hold values from -6 to 6
- entering_mixer_sections: bfloat16 [2, 8192, 1024], P(None, 'chan'), may hold values from -0.125 to 0.125
- sigmoid_switch_matrix: bfloat16 [4096, 1024], P('chan'), may hold values from -0.1875 to 0.1875
- leaving_mixer_sections: bfloat16 [2, 8192, 1024], P(None, 'chan'), may hold values from -0.125 to 0.125
- channel_persistence: float32 [4096], P('chan'), may hold values from 0.96 to 1, as said below
- position_boosts: float32 [8192], P('seq'), may hold values from 0.5 to 1, as said below
- result_cotangent: bfloat16 [8192, 4096], P('seq', 'chan'), may hold values from -6 to 6
Outputs:
- layer_out: bfloat16 [8192, 4096], P('seq', 'chan')
- token_grads: bfloat16 [8192, 4096], P('seq', 'chan')
- in_grads: float32 [2, 8192, 1024], P(None, ('chan', 'seq'))
- out_grads: float32 [2, 8192, 1024], P(None, ('chan', 'seq'))
- gate_grads: float32 [4096, 1024], P(('chan', 'seq'))
Inputs may be any that keep to these rules, and one draw needn't show every extreme that they name: `channel_persistence`: each entry is positive and below one. `position_boosts`: each entry is positive and at most one.
All inputs are finite; a program needn't handle non-finite values.
Results may differ from a plain program's by a relative error of at most 0.027.
Values may be sent and summed in bfloat16 or wider, within the bound.
A program may use at most 192 MiB of HBM per device.

v0:
```python
import functools

import jax
import jax.numpy as jnp
from jax import lax
from jax.experimental import pallas as pl
from jax.experimental.pallas import tpu as pltpu
from jax.sharding import PartitionSpec as P

SEGMENTS = 32
LANES = 128
MESH = pl.DeviceIdType.MESH
F32, BF16 = jnp.float32, jnp.bfloat16


def from_partner(block, axis, distance):
    count = lax.axis_size(axis)
    route = []
    for low in range(count):
        high = low | 1 << distance
        if high != low and high < count:
            route += [(low, high), (high, low)]
    return lax.ppermute(block, axis, route)


def dot(left, right):
    return jnp.dot(left, right, preferred_element_type=jnp.float32)


def dot_rows(left, right):
    return lax.dot_general(
        left, right, (((0,), (0,)), ((), ())), preferred_element_type=jnp.float32
    )


def dot_trans(left, right):
    return lax.dot_general(
        left, right, (((1,), (1,)), ((), ())), preferred_element_type=jnp.float32
    )


def every(ref, step):
    return ref[pl.ds(step, SEGMENTS, stride=ref.shape[0] // SEGMENTS), :]


def ends_kernel(drive, out_cot, gate, keep, boosts, seg_ref, tot_ref, x_ref, g_ref):
    lam = keep[...]
    scale = jnp.sqrt(1.0 - lam * lam)
    x_ref[...] = scale * drive[...].astype(jnp.float32)
    g_ref[...] = out_cot[...] * gate[...]
    steps = x_ref.shape[0] // SEGMENTS
    shape = (SEGMENTS, LANES)
    lam = jnp.broadcast_to(lam, shape)
    state = jnp.zeros(shape, jnp.float32)
    prod = jnp.ones(shape, jnp.float32)
    for i in range(steps):
        a = every(boosts, i) * lam
        state = a * state + every(x_ref, i)
        prod = a * prod
    back = jnp.zeros(shape, jnp.float32)
    for i in reversed(range(steps)):
        a = every(boosts, i) * lam
        back = a * (every(g_ref, i) + back)
    seg_ref[0] = prod
    seg_ref[1] = state
    seg_ref[2] = back
    p = jnp.ones((1, LANES), jnp.float32)
    h = jnp.zeros((1, LANES), jnp.float32)
    c = jnp.zeros((1, LANES), jnp.float32)
    for s in range(SEGMENTS):
        here = prod[s : s + 1]
        h = here * h + state[s : s + 1]
        p = here * p
        r = SEGMENTS - 1 - s
        c = prod[r : r + 1] * c + back[r : r + 1]
    tot_ref[0] = p
    tot_ref[1] = h
    tot_ref[2] = c


def run_kernel(
    devices, drive, out_cot, gate, keep, boosts, seg, tots, place,
    mixed, gate_pre, drive_grad, x_ref, g_ref, start_ref, stop_ref,
):
    lam = keep[...]
    scale = jnp.sqrt(1.0 - lam * lam)
    x_ref[...] = scale * drive[...].astype(jnp.float32)
    g_ref[...] = out_cot[...] * gate[...]
    steps = x_ref.shape[0] // SEGMENTS
    shape = (SEGMENTS, LANES)
    here = place[...]
    h = jnp.zeros((1, LANES), jnp.float32)
    c = jnp.zeros((1, LANES), jnp.float32)
    for k in range(devices):
        h = jnp.where(k < here, tots[k, 0] * h + tots[k, 1], h)
        r = devices - 1 - k
        c = jnp.where(r > here, tots[r, 0] * c + tots[r, 2], c)
    for s in range(SEGMENTS):
        start_ref[s : s + 1] = h
        h = seg[0, s : s + 1] * h + seg[1, s : s + 1]
        r = SEGMENTS - 1 - s
        stop_ref[r : r + 1] = c
        c = seg[0, r : r + 1] * c + seg[2, r : r + 1]
    lam = jnp.broadcast_to(lam, shape)
    state = start_ref[...]
    back = stop_ref[...]
    for i in range(steps):
        state = every(boosts, i) * lam * state + every(x_ref, i)
        x_ref[pl.ds(i, SEGMENTS, stride=steps), :] = state
        r = steps - 1 - i
        total = every(g_ref, r) + back
        g_ref[pl.ds(r, SEGMENTS, stride=steps), :] = total
        back = every(boosts, r) * lam * total
    sig = gate[...]
    product = x_ref[...] * sig
    mixed[...] = product.astype(jnp.bfloat16)
    gate_pre[...] = (out_cot[...] * product * (1.0 - sig)).astype(jnp.bfloat16)
    drive_grad[...] = (scale * g_ref[...]).astype(jnp.bfloat16)


def recurrences(drive, out_cot, gate, keep, boosts):
    tokens, width = drive.shape
    devices = lax.axis_size("seq")
    keep = keep[None, :]
    boosts = jnp.broadcast_to(boosts[:, None], (tokens, LANES))
    big = pl.BlockSpec((tokens, LANES), lambda j: (0, j))
    row = pl.BlockSpec((1, LANES), lambda j: (0, j))
    same = pl.BlockSpec((tokens, LANES), lambda j: (0, 0))
    seg_spec = pl.BlockSpec((3, SEGMENTS, LANES), lambda j: (0, 0, j))
    scratch = pltpu.VMEM((tokens, LANES), jnp.float32)
    small = pltpu.VMEM((SEGMENTS, LANES), jnp.float32)
    area = tokens * width
    seg, totals = pl.pallas_call(
        ends_kernel,
        grid=(width // LANES,),
        in_specs=[big, big, big, row, same],
        out_specs=[seg_spec, pl.BlockSpec((3, 1, LANES), lambda j: (0, 0, j))],
        out_shape=[
            jax.ShapeDtypeStruct((3, SEGMENTS, width), jnp.float32),
            jax.ShapeDtypeStruct((3, 1, width), jnp.float32),
        ],
        scratch_shapes=[scratch, scratch],
        compiler_params=pltpu.CompilerParams(vmem_limit_bytes=24 << 20),
        cost_estimate=pl.CostEstimate(flops=10 * area, bytes_accessed=10 * area, transcendentals=0),
        name="ends",
    )(drive, out_cot, gate, keep, boosts)
    totals = lax.all_gather(totals, "seq")
    place = jnp.full((1, LANES), lax.axis_index("seq"), jnp.int32)
    return pl.pallas_call(
        functools.partial(run_kernel, devices),
        grid=(width // LANES,),
        in_specs=[
            big, big, big, row, same, seg_spec,
            pl.BlockSpec((devices, 3, 1, LANES), lambda j: (0, 0, 0, j)),
            pl.BlockSpec((1, LANES), lambda j: (0, 0)),
        ],
        out_specs=[big, big, big],
        out_shape=[jax.ShapeDtypeStruct((tokens, width), jnp.bfloat16)] * 3,
        scratch_shapes=[scratch, scratch, small, small],
        compiler_params=pltpu.CompilerParams(vmem_limit_bytes=24 << 20),
        cost_estimate=pl.CostEstimate(flops=20 * area, bytes_accessed=16 * area, transcendentals=0),
        name="recurrences",
    )(drive, out_cot, gate, keep, boosts, seg, totals, place)


SLOTS = 4
FLIGHT = 2


def after_kernel(levels, chips, scale, *refs):
    it = iter(refs)
    z = [next(it) for _ in range(levels)]
    zm = [next(it) for _ in range(levels)]
    e = [None] + [next(it) for _ in range(levels)]
    mixed, gate_pre, drive_grad, entering, leaving, switch = (next(it) for _ in range(6))
    layer_out, token_grads, in_grads, out_grads, gate_grads = (next(it) for _ in range(5))
    stage, part, sums, gate_sums, right, left, gate_right, gate_left = (next(it) for _ in range(8))
    mates, shares, outs, cots, sent, final = (next(it) for _ in range(6))
    load_sem, sib_send, sib_recv, right_send, right_recv, left_send, left_recv = (
        next(it) for _ in range(7)
    )
    swap_send, swap_recv, final_sem, store_sem = (next(it) for _ in range(4))

    tokens, width = mixed.shape
    half = width // 2
    seq, chan = lax.axis_index("seq"), lax.axis_index("chan")
    zi, core = lax.div(seq, 2), lax.rem(seq, 2)
    zo = chips - 1 - zi
    sibling = {"seq": seq + 1 - 2 * core}
    upper, lower = {"seq": seq + 2}, {"seq": seq - 2}

    def partner(level):
        d = 1 << level
        bit = lax.rem(lax.div(chan, d), 2)
        return {"chan": chan + d * (1 - 2 * bit)}

    barrier = pltpu.get_barrier_semaphore()

    def greet(device):
        pl.semaphore_signal(barrier, inc=1, device_id=device, device_id_type=MESH)

    for level in range(levels):
        greet(partner(level))
    greet(sibling)

    for device in (lax.rem(seq + 2, 2 * chips), lax.rem(seq + 2 * chips - 2, 2 * chips)):
        greet({"seq": device})
    pl.semaphore_wait(barrier, levels + 3)

    def remote(source, target, send, recv, device):
        return pltpu.make_async_remote_copy(
            src_ref=source, dst_ref=target, send_sem=send, recv_sem=recv,
            device_id=device, device_id_type=MESH,
        )

    def swap_out(step, source):
        return remote(source, mates.at[step], swap_send.at[step], swap_recv.at[step], partner(step))

    def swap_back(step):
        n = levels + step
        return remote(
            sent, shares.at[step], swap_send.at[n], swap_recv.at[n], partner(levels - 1 - step)
        )

    groups = [(gate_grads, gate_sums, gate_right, gate_left)]
    for step in range(levels):
        for out in (in_grads.at[levels - 1 - step], out_grads.at[step]):
            n = len(groups) - 1
            groups.append((out, sums.at[n], right.at[n], left.at[n]))

    def hop(g, k, h, way):
        _, total, up, down = groups[g]
        rows = up.shape[1]
        cols = pl.ds(h * half, half)
        into = (up, down)[way]
        at = (0 if way else chips - k) if k > 0 else 0
        if way:
            first = total.at[pl.ds((k - 1) * rows, rows), cols]
            send, recv, device = left_send, left_recv, lower
        else:
            first = total.at[pl.ds((chips - k) * rows, rows), cols]
            send, recv, device = right_send, right_recv, upper
        n = (g * (chips - 1) + k - 1) * 2 + h

        def copy(source):
            return remote(source, into.at[k - 1, :, cols], send.at[n], recv.at[n], device)

        later = into.at[k - 2, :, cols] if k > 1 else None
        return copy, first, later

    issued = []

    def finish_send(key):
        g, k, h = key
        for way, place in ((0, zi), (1, zo)):
            @pl.when(place <= k - 1)
            def _(way=way):
                copy, first, _ = hop(g, k, h, way)
                copy(first).wait_send()

    def send(g, k, h):
        if len(issued) >= FLIGHT:
            finish_send(issued[-FLIGHT])
        issued.append((g, k, h))
        for way, place in ((0, zi), (1, zo)):
            copy, first, later = hop(g, k, h, way)

            @pl.when(place == 0)
            def _(copy=copy, first=first):
                copy(first).start()

            if k > 1:
                @pl.when((place >= 1) & (place <= k - 1))
                def _(copy=copy, later=later):
                    copy(later).start()

    def event(g, k, h):
        out, total, up, down = groups[g]
        rows = up.shape[1]
        cols = pl.ds(h * half, half)
        for way, place in ((0, zi), (1, zo)):
            copy, first, _ = hop(g, k, h, way)

            @pl.when((place >= 1) & (place <= k))
            def _(way=way, copy=copy, first=first):
                copy(first).wait_recv()
                if k < chips - 1:
                    shard = zi - 1 + chips - k
                    if way:
                        shard = chips - 1 - (zo - 1 + chips - k)
                    at = pl.ds(pl.multiple_of(shard * rows, rows), rows)
                    into = (up, down)[way]
                    into[k - 1, :, cols] = (
                        into[k - 1, :, cols].astype(F32) + total[at, cols].astype(F32)
                    ).astype(BF16)

        if k < chips - 1:
            send(g, k + 1, h)
            return
        slot = g % 2
        if h == 0 and g >= 2:
            final_copy(g - 2).wait()
        at = pl.ds(pl.multiple_of(zi * rows, rows), rows)
        final[slot, :rows, cols] = total[at, cols].astype(F32) * scale

        @pl.when(zi > 0)
        def _():
            final[slot, :rows, cols] += up[chips - 2, :, cols].astype(F32) * scale

        @pl.when(zo > 0)
        def _():
            final[slot, :rows, cols] += down[chips - 2, :, cols].astype(F32) * scale

        if h == 1:
            final_copy(g).start()

    def final_copy(g):
        out, _, up, _ = groups[g]
        rows = up.shape[1]
        return pltpu.make_async_copy(final.at[g % 2, :rows], out, final_sem.at[g % 2])

    blocks = []

    def sibling_copy(b):
        g, offset, slot = blocks[b]
        total = groups[g][1]
        return remote(
            part.at[slot, 1 - core], total.at[pl.ds(offset, half)],
            sib_send.at[b], sib_recv.at[b], sibling,
        )

    def grad(g, offset, left_ref, right_ref):
        b = len(blocks)
        blocks.append((g, offset, b % 2))
        slot = b % 2
        if b >= 2:
            sibling_copy(b - 2).wait_send()
        rows = groups[g][2].shape[1]
        tile = min(256, width)

        @pl.loop(0, width // tile)
        def _(i):
            cols = pl.ds(pl.multiple_of(i * tile, tile), tile)
            result = dot_rows(left_ref[:, cols], right_ref[...]).astype(BF16)
            pieces = tile // rows
            if pieces <= 1:
                per = rows // tile
                shard = lax.div(i, per)
                at = lax.div(shard, 2) * rows + lax.rem(i, per) * tile
                part[slot, lax.rem(shard, 2), pl.ds(pl.multiple_of(at, tile), tile), :] = result
            else:
                for q in range(pieces):
                    at = i * (tile // 2) + q // 2 * rows
                    part[slot, q % 2, pl.ds(pl.multiple_of(at, rows), rows), :] = (
                        result[q * rows : (q + 1) * rows]
                    )

        sibling_copy(b).start()
        return b

    def chip_sum(b):
        g, offset, slot = blocks[b]
        total = groups[g][1]
        sibling_copy(b).wait_recv()
        tile = min(128, half)

        @pl.loop(0, half // tile)
        def _(i):
            at = pl.multiple_of(i * tile, tile)
            there = pl.ds(offset + at, tile)
            total[there, :] = (
                total[there, :].astype(F32) + part[slot, core, pl.ds(at, tile), :].astype(F32)
            ).astype(BF16)

    work = []
    tall = min(256, tokens)

    def tiles(store):
        @pl.loop(0, tokens // tall)
        def _(i):
            store(pl.ds(pl.multiple_of(i * tall, tall), tall))

    def task(loads, run):
        work.append((loads, run))

    def top(weights, level):
        return weights.at[level, pl.ds(0, width)]

    def bot(weights, level):
        return weights.at[level, pl.ds(width, width)]

    queue = []
    pending = []

    def settle():
        while pending:
            b, group_done = pending.pop(0)
            chip_sum(b)
            if group_done:
                g = blocks[b][0]
                for k in range(1, chips):
                    for h in range(2):
                        queue.append((g, k, h))

    started = set()

    def begin():
        for g, k, h in list(queue):
            if k == 1 and (g, h) not in started:
                ahead = queue.index((g, k, h))
                if ahead <= 1:
                    started.add((g, h))
                    send(g, 1, h)

    def pump(count):
        begin()
        for _ in range(count):
            if not queue:
                return
            event(*queue.pop(0))
            begin()

    def drain(keep):
        pump(max(len(queue) - keep, 0))

    def grad_task(g, offset, left_ref, right_ref, last):
        fixed = [r for r in (left_ref, right_ref) if isinstance(r, tuple)]
        loads = [r[0] for r in fixed]

        def run(bufs):
            bufs = list(bufs)
            lhs = bufs.pop(0) if isinstance(left_ref, tuple) else left_ref
            rhs = bufs.pop(0) if isinstance(right_ref, tuple) else right_ref
            settle()
            pending.append((grad(g, offset, lhs, rhs), last))
            pump(1)

        task(loads, run)

    def hbm(ref):
        return (ref,)

    def share_task(step):
        down = levels - 1 - step
        loads = [bot(entering, down)]
        if step == 0:
            loads = [drive_grad] + loads

        def run(bufs):
            cot = bufs[0] if step == 0 else cots.at[step - 1]
            weight = bufs[-1]
            if step > 0:
                swap_back(step - 1).wait_send()

            def store(at):
                sent[at, :] = dot_trans(cot[at, :], weight[...]).astype(BF16)

            tiles(store)
            swap_back(step).start()
            settle()
            pump(1)

        task(loads, run)

    def wait_task(fn, keep):
        def run(bufs):
            settle()
            drain(keep)
            fn()

        task([], run)

    def out_task(step):
        loads = [top(leaving, step), bot(leaving, step)]
        last = step == levels - 1
        if step == 0:
            loads.append(mixed)
        if last:
            loads.append(z[0])

        def run(bufs):
            held = bufs[2] if step == 0 else outs.at[step - 1]
            mate = mates.at[step]

            def store(at):
                total = dot(held[at, :], bufs[0][...]) + dot(mate[at, :], bufs[1][...])
                if last:
                    mates[0, at, :] = (bufs[-1][at, :].astype(F32) + total).astype(BF16)
                else:
                    outs[step, at, :] = total.astype(BF16)

            tiles(store)
            if last:
                pltpu.make_async_copy(mates.at[0], layer_out, store_sem.at[0]).start()
            else:
                swap_out(step + 1, outs.at[step]).start()
            settle()
            pump(1)

        task(loads, run)

    def back_task(step):
        down = levels - 1 - step
        last = step == levels - 1
        loads = [top(entering, down)]
        if step == 0:
            loads.append(drive_grad)
        if last:
            loads += [gate_pre, switch, e[levels]]

        def run(bufs):
            cot = bufs[1] if step == 0 else cots.at[step - 1]

            def store(at):
                total = dot_trans(cot[at, :], bufs[0][...]) + shares[step, at, :].astype(F32)
                if last:
                    total = total + dot_trans(bufs[-3][at, :], bufs[-2][...])
                    total = total + bufs[-1][at, :].astype(F32)
                    shares[0, at, :] = total.astype(BF16)
                else:
                    cots[step, at, :] = total.astype(BF16)

            tiles(store)
            if last:
                pltpu.make_async_copy(shares.at[0], token_grads, store_sem.at[1]).start()
            settle()
            pump(1)

        task(loads, run)

    swap_out(0, mixed).start()
    share_task(0)
    grad_task(0, 0, hbm(z[0]), hbm(gate_pre), True)
    for step in range(levels):
        down = levels - 1 - step
        g = 1 + 2 * step
        cot = hbm(drive_grad) if step == 0 else cots.at[step - 1]
        held = hbm(mixed) if step == 0 else outs.at[step - 1]
        grad_task(g, 0, hbm(z[down]), cot, False)
        grad_task(g, half, hbm(zm[down]), cot, True)
        grad_task(g + 1, 0, held, hbm(e[step + 1]), False)
        wait_task(lambda step=step: swap_out(step, mixed).wait_recv(), 3)
        grad_task(g + 1, half, mates.at[step], hbm(e[step + 1]), True)
        out_task(step)
        wait_task(lambda step=step: swap_back(step).wait_recv(), 1 << 20)
        back_task(step)
        if step < levels - 1:
            share_task(step + 1)

    spans, count = [], 0
    for loads, _ in work:
        spans.append((count, count + len(loads)))
        count += len(loads)
    flat = [ref for loads, _ in work for ref in loads]
    owner = [t for t, (loads, _) in enumerate(work) for _ in loads]

    def load(n):
        rows = flat[n].shape[0]
        return pltpu.make_async_copy(
            flat[n], stage.at[n % SLOTS, pl.ds(0, rows)], load_sem.at[n % SLOTS]
        )

    ahead = 0
    for t, (loads, run) in enumerate(work):
        while ahead < count and (ahead < SLOTS or owner[ahead - SLOTS] < t):
            load(ahead).start()
            ahead += 1
        first, last = spans[t]
        for n in range(first, last):
            load(n).wait()
        run([stage.at[n % SLOTS, pl.ds(0, flat[n].shape[0])] for n in range(first, last)])
    settle()
    drain(0)
    for key in issued[-FLIGHT:]:
        finish_send(key)
    for b in (len(blocks) - 2, len(blocks) - 1):
        sibling_copy(b).wait_send()
    for g in (len(groups) - 2, len(groups) - 1):
        final_copy(g).wait()
    for step in range(levels):
        swap_out(step, mixed).wait_send()
    swap_back(levels - 1).wait_send()
    pltpu.make_async_copy(mates.at[0], layer_out, store_sem.at[0]).wait()
    pltpu.make_async_copy(shares.at[0], token_grads, store_sem.at[1]).wait()


def after_scan(z, z_mates, e, mixed, gate_pre, drive_grad, entering, leaving, switch, scale):
    levels = len(z)
    tokens, width = mixed.shape
    seq = lax.axis_size("seq")
    chips = seq // 2
    groups, blocks = 1 + 2 * levels, 1 + 4 * levels
    rows = 2 * width // seq
    hops = groups * (chips - 1) * 2
    hbm = pl.BlockSpec(memory_space=pl.ANY)
    dma = pltpu.SemaphoreType.DMA
    args = [*z, *z_mates, *e, mixed, gate_pre, drive_grad, entering, leaving, switch]
    square = width * width
    count = 2 * tokens * square * (4 * levels + 1 + 4 * levels + 1)
    return pl.pallas_call(
        functools.partial(after_kernel, levels, chips, scale),
        in_specs=[hbm] * len(args),
        out_specs=[hbm] * 5,
        out_shape=[
            jax.ShapeDtypeStruct((tokens, width), BF16),
            jax.ShapeDtypeStruct((tokens, width), BF16),
            jax.ShapeDtypeStruct((levels, rows, width), F32),
            jax.ShapeDtypeStruct((levels, rows, width), F32),
            jax.ShapeDtypeStruct((rows // 2, width), F32),
        ],
        scratch_shapes=[
            pltpu.VMEM((SLOTS, max(tokens, width), width), BF16),
            pltpu.VMEM((2, 2, width // 2, width), BF16),
            pltpu.VMEM((2 * levels, width, width), BF16),
            pltpu.VMEM((width // 2, width), BF16),
            pltpu.VMEM((2 * levels, chips - 1, rows, width), BF16),
            pltpu.VMEM((2 * levels, chips - 1, rows, width), BF16),
            pltpu.VMEM((chips - 1, rows // 2, width), BF16),
            pltpu.VMEM((chips - 1, rows // 2, width), BF16),
            pltpu.VMEM((levels, tokens, width), BF16),
            pltpu.VMEM((levels, tokens, width), BF16),
            pltpu.VMEM((levels - 1, tokens, width), BF16),
            pltpu.VMEM((levels - 1, tokens, width), BF16),
            pltpu.VMEM((tokens, width), BF16),
            pltpu.VMEM((2, rows, width), F32),
            dma((SLOTS,)), dma((blocks,)), dma((blocks,)),
            dma((hops,)), dma((hops,)), dma((hops,)), dma((hops,)),
            dma((2 * levels,)), dma((2 * levels,)), dma((2,)), dma((2,)),
        ],
        compiler_params=pltpu.CompilerParams(
            collective_id=0, has_side_effects=True, vmem_limit_bytes=60 << 20
        ),
        cost_estimate=pl.CostEstimate(
            flops=count, bytes_accessed=60 * tokens * width, transcendentals=0
        ),
        name="after_scan",
    )(*args)


def share_of(cotangent, weight):
    return dot_trans(cotangent, weight[cotangent.shape[1] :]).astype(jnp.bfloat16)


def transposed_step(cotangent, weight, received):
    width = cotangent.shape[1]
    return dot_trans(cotangent, weight[:width]) + received.astype(jnp.float32)


def shards(
    layer_source,
    entering,
    switch,
    leaving,
    channel_persistence,
    position_boosts,
    result_cotangent,
):
    levels = entering.shape[0]
    width = layer_source.shape[1]
    scale = float(layer_source.shape[0] * lax.axis_size("seq")) ** (-0.5)

    z, z_mates = [layer_source], []
    e = [None] * levels + [result_cotangent]
    for step in range(levels):
        z_mates.append(from_partner(z[step], "chan", step))
        down = levels - 1 - step
        share = from_partner(share_of(e[down + 1], leaving[down]), "chan", down)
        e[down] = transposed_step(e[down + 1], leaving[down], share)
        if down > 0:
            e[down] = e[down].astype(jnp.bfloat16)
        summed = dot(z[step], entering[step, :width]) + dot(z_mates[step], entering[step, width:])
        z.append(summed.astype(jnp.bfloat16))
    gate = jax.nn.sigmoid(dot(layer_source, switch))

    mixed, gate_pre_grad, drive_grad = recurrences(
        z[levels], e[0], gate, channel_persistence, position_boosts
    )
    return after_scan(
        z[:levels], z_mates, e[1:], mixed, gate_pre_grad, drive_grad,
        entering, leaving, switch, scale,
    )


def solution(mesh):
    placed = (
        P("seq", "chan"),
        P(None, "chan", None),
        P("chan", None),
        P(None, "chan", None),
        P("chan"),
        P("seq"),
        P("seq", "chan"),
    )
    return jax.shard_map(
        shards,
        mesh=mesh,
        in_specs=placed,
        out_specs=(
            P("seq", "chan"),
            P("seq", "chan"),
            P(None, ("chan", "seq"), None),
            P(None, ("chan", "seq"), None),
            P(("chan", "seq"), None),
        ),
        check_vma=False,
    )
```

profile of v0, /device:TPU:8, one launch (start us, length us, event | category | flops | bytes accessed | tf_op | source)
XLA Modules:
  0.0 362.8 jit_solution(10417095784795294178)
XLA Ops:
  0.6 6.1 %fusion.26 = bf16[1024,1024]{1,0:T(8,128)(2,1)} fusion(bf16[1024,1024]{1,0:T(8,128)(2,1)} %refs_5_.1, bf16[2,2048,1024]{2,1,0:T(8,128)(2,1)} %refs_10_.1), kind=kOutput, calls=%fused_computation.29 | convolution fusion | flops 2148532224 | bytes 6291456 | tf_op jit(solution)/shard_map/dot_general | solution.py:37
  6.7 1.5 collective-permute-start.2
  8.2 1.5 collective-permute-start
  9.7 4.1 %fusion.14 = f32[1024,1024]{1,0:T(8,128)S(1)} fusion(bf16[1024,1024]{1,0:T(8,128)(2,1)S(1)} %copy-done.10, bf16[2,2048,1024]{2,1,0:T(8,128)(2,1)} %refs_9_.1), kind=kOutput, calls=%fused_computation.19 | convolution fusion | flops 2147483648 | bytes 8388608 | tf_op jit(solution)/shard_map/dot_general | solution.py:27
  13.8 40.6 %collective-permute-done.2 = bf16[1024,1024]{1,0:T(8,128)(2,1)} collective-permute-done((bf16[1024,1024]{1,0:T(8,128)(2,1)}, bf16[1024,1024]{1,0:T(8,128)(2,1)}, u32[]{:S(2)}, u32[]{:S(2)}) %collective-permute-start.2) | collective-permute-done | bytes 2097184 | tf_op jit(solution)/shard_map/ppermute | solution.py:23
  54.4 4.0 %add_convert_fusion.1.refs_4_ = bf16[1024,1024]{1,0:T(8,128)(2,1)S(1)} fusion(bf16[1024,1024]{1,0:T(8,128)(2,1)} %collective-permute-done.2, bf16[1024,1024]{1,0:T(8,128)(2,1)S(1)} %copy-done.11, bf16[2,2048,1024]{2,1,0:T(8,128)(2,1)S(1)} %copy-done.9), kind=kOutput, calls=%fused_computation.3 | convolution fusion | flops 2150629376 | bytes 8388608 | tf_op jit(solution)/shard_map/dot_general | solution.py:37
  59.7 2.4 fusion.29
  62.1 1.6 collective-permute-start.3
  63.7 3.9 %add_convert_fusion.2.refs_1_ = bf16[1024,1024]{1,0:T(8,128)(2,1)S(1)} fusion(f32[1024,1024]{1,0:T(8,128)S(1)} %fusion.14, bf16[1024,1024]{1,0:T(8,128)(2,1)} %collective-permute-done.refs_2_, bf16[2,2048,1024]{2,1,0:T(8,128)(2,1)S(1)} %bitcast.52), kind=kOutput, calls=%fused_computation.4 | convolution fusion | flops 2149580800 | bytes 10485760 | tf_op jit(solution)/shard_map/dot_general | solution.py:27
  67.6 1.6 collective-permute-start.1
  69.2 2.7 add_divide_fusion.gate
  72.0 2.6 fusion.6
  74.6 34.0 %collective-permute-done.3 = bf16[1024,1024]{1,0:T(8,128)(2,1)S(1)} collective-permute-done((bf16[1024,1024]{1,0:T(8,128)(2,1)S(1)}, bf16[1024,1024]{1,0:T(8,128)(2,1)S(1)}, u32[]{:S(2)}, u32[]{:S(2)}) %collective-permute-start.3) | collective-permute-done | bytes 2097184 | tf_op jit(solution)/shard_map/ppermute | solution.py:23
  108.7 2.4 convert_add_fusion.out_cot
  111.1 2.8 collective-permute-done.1.refs_3_
  113.9 2.4 add_convert_fusion.drive
  116.5 10.4 %ends.1 = (f32[3,32,1024]{2,1,0:T(8,128)S(1)}, f32[3,1,1024]{2,1,0:T(1,128)S(1)}) custom-call(bf16[1024,1024]{1,0:T(8,128)(2,1)S(1)} %add_convert_fusion.drive, f32[1024,1024]{1,0:T(8,128)S(1)} %convert_add_fusion.out_cot, f32[1024,1024]{1,0:T(8,128)S(1)} %add_divide_fusion.gate, f32[1,1024]{1,0:T(1,128)S(1)} %bitcast.49, ...), custom_call_target="tpu_custom_call" | custom-call | flops 10485760 | bytes 10485760 | tf_op jit(solution)/shard_map/ends/pallas_call | solution.py:133
  126.9 14.1 %all-gather = f32[24,1,1024]{2,1,0:T(1,128)S(1)} all-gather(f32[3,1,1024]{2,1,0:T(1,128)S(1)} %get-tuple-element.11), channel_id=2, replica_groups=mesh['seq'=8,'chan'=4] {'seq'}, dimensions={0}, use_global_device_ids=true | all-gather | bytes 110592 | tf_op jit(solution)/shard_map/all_gather | solution.py:147
  141.0 22.6 %recurrences.1 = (bf16[1024,1024]{1,0:T(8,128)(2,1)S(1)}, bf16[1024,1024]{1,0:T(8,128)(2,1)S(1)}, bf16[1024,1024]{1,0:T(8,128)(2,1)S(1)}) custom-call(bf16[1024,1024]{1,0:T(8,128)(2,1)S(1)} %add_convert_fusion.drive, f32[1024,1024]{1,0:T(8,128)S(1)} %convert_add_fusion.out_cot, f32[1024,1024]{1,0:T(8,128)S(1)} %add_divide_fusion.gate, ...), custom_call_target="tpu_custom_call" | custom-call | flops 20971520 | bytes 16777216 | tf_op jit(solution)/shard_map/recurrences/pallas_call | solution.py:149
  166.2 1.4 copy-done.3
  167.6 184.9 %after_scan.1 = (bf16[1024,1024]{1,0:T(8,128)(2,1)}, bf16[1024,1024]{1,0:T(8,128)(2,1)}, f32[2,256,1024]{2,1,0:T(8,128)}, f32[2,256,1024]{2,1,0:T(8,128)}, f32[128,1024]{1,0:T(8,128)}) custom-call(bf16[1024,1024]{1,0:T(8,128)(2,1)} %refs_0_.1, bf16[1024,1024]{1,0:T(8,128)(2,1)} %copy-done.13, bf16[1024,1024]{1,0:T(8,128)(2,1)} %collective-permute-done.refs_2_, ...), custom_call_target="tpu_custom_call" | custom-call | flops 38654705664 | bytes 62914560 | tf_op jit(solution)/shard_map/after_scan/pallas_call | solution.py:600
  352.5 3.2 copy.17
  355.7 1.3 copy.18
  358.1 1.3 copy.19
  (43 shorter events, 8.4 us)
Async XLA Ops:
  0.6 7.6 %copy-start.10 = (bf16[1024,1024]{1,0:T(8,128)(2,1)S(1)}, bf16[1024,1024]{1,0:T(8,128)(2,1)}, u32[]{:S(2)}) copy-start(bf16[1024,1024]{1,0:T(8,128)(2,1)} %refs_0_.1) | copy-start | bytes 6291460
  6.7 47.7 %collective-permute-start.2 = (bf16[1024,1024]{1,0:T(8,128)(2,1)}, bf16[1024,1024]{1,0:T(8,128)(2,1)}, u32[]{:S(2)}, u32[]{:S(2)}) collective-permute-start(bf16[1024,1024]{1,0:T(8,128)(2,1)} %fusion.26), channel_id=1, source_target_pairs={{0,2},{2,0},{1,3},{3,1},{4,6},{6,4},{5,7},{7,5},{8,10},{10,8},{9,1... | collective-permute-start | bytes 6291464 | tf_op jit(solution)/shard_map/ppermute | solution.py:23
  8.2 55.4 %collective-permute-start = (bf16[1024,1024]{1,0:T(8,128)(2,1)S(1)}, bf16[1024,1024]{1,0:T(8,128)(2,1)}, u32[]{:S(2)}, u32[]{:S(2)}) collective-permute-start(bf16[1024,1024]{1,0:T(8,128)(2,1)S(1)} %copy-done.10), channel_id=1, source_target_pairs={{0,1},{1,0},{2,3},{3,2},{4,5},{5,4},{6,7},{7,6},{8,9},{9,8},{10,11... | collective-permute-start | bytes 6291464 | tf_op jit(solution)/shard_map/ppermute | solution.py:23
  9.7 44.7 %copy-start.9 = (bf16[2,2048,1024]{2,1,0:T(8,128)(2,1)S(1)}, bf16[2,2048,1024]{2,1,0:T(8,128)(2,1)}, u32[]{:S(2)}) copy-start(bf16[2,2048,1024]{2,1,0:T(8,128)(2,1)} %refs_10_.1) | copy-start | bytes 25165828
  9.7 44.7 %copy-start.11 = (bf16[1024,1024]{1,0:T(8,128)(2,1)S(1)}, bf16[1024,1024]{1,0:T(8,128)(2,1)}, u32[]{:S(2)}) copy-start(bf16[1024,1024]{1,0:T(8,128)(2,1)} %refs_5_.1) | copy-start | bytes 6291460
  9.7 53.9 %slice-start = ((s8[8388608]{0:T(1024)(128)(4,1)}), s8[4194304]{0:T(1024)(128)(4,1)S(1)}, s32[]{:S(2)}) async-start(s8[8388608]{0:T(1024)(128)(4,1)} %bitcast.51), calls=%async_computation | async-start | bytes 8388608
  13.8 49.9 %slice-start.1 = ((s8[8388608]{0:T(1024)(128)(4,1)}), s8[4194304]{0:T(1024)(128)(4,1)S(1)}, s32[]{:S(2)}) async-start(s8[8388608]{0:T(1024)(128)(4,1)} %bitcast.51), calls=%async_computation.1 | async-start | bytes 8388608
  58.4 1.3 copy-start.15
  62.1 7.1 %copy-start.12 = (bf16[1024,1024]{1,0:T(8,128)(2,1)S(1)}, bf16[1024,1024]{1,0:T(8,128)(2,1)}, u32[]{:S(2)}) copy-start(bf16[1024,1024]{1,0:T(8,128)(2,1)} %refs_11_.1) | copy-start | bytes 6291460
  62.1 46.6 %collective-permute-start.3 = (bf16[1024,1024]{1,0:T(8,128)(2,1)S(1)}, bf16[1024,1024]{1,0:T(8,128)(2,1)S(1)}, u32[]{:S(2)}, u32[]{:S(2)}) collective-permute-start(bf16[1024,1024]{1,0:T(8,128)(2,1)S(1)} %fusion.29), channel_id=1, source_target_pairs={{0,1},{1,0},{2,3},{3,2},{4,5},{5,4},{6,7},{7,6},{8,9},{9,8},{10,11... | collective-permute-start | bytes 6291464 | tf_op jit(solution)/shard_map/ppermute | solution.py:23
  67.6 4.3 %copy-start.13 = (bf16[1024,1024]{1,0:T(8,128)(2,1)}, bf16[1024,1024]{1,0:T(8,128)(2,1)S(1)}, u32[]{:S(2)}) copy-start(bf16[1024,1024]{1,0:T(8,128)(2,1)S(1)} %add_convert_fusion.2.refs_1_) | copy-start | bytes 6291460
  67.6 46.3 %collective-permute-start.1 = (bf16[1024,1024]{1,0:T(8,128)(2,1)S(1)}, bf16[1024,1024]{1,0:T(8,128)(2,1)S(1)}, u32[]{:S(2)}, u32[]{:S(2)}) collective-permute-start(bf16[1024,1024]{1,0:T(8,128)(2,1)S(1)} %add_convert_fusion.2.refs_1_), channel_id=1, source_target_pairs={{0,2},{2,0},{1,3},{3,1},{4,6},{6,4},{5,7},{7,5},{8,10},{10,8},{9,1... | collective-permute-start | bytes 6291464 | tf_op jit(solution)/shard_map/ppermute | solution.py:23
  72.0 36.7 %copy-start.16 = (bf16[1024,1024]{1,0:T(8,128)(2,1)S(1)}, bf16[1024,1024]{1,0:T(8,128)(2,1)}, u32[]{:S(2)}) copy-start(bf16[1024,1024]{1,0:T(8,128)(2,1)} %copy-done.15) | copy-start | bytes 6291460
  111.1 5.2 %copy-start.8 = (f32[1024]{0:T(1024)S(1)}, f32[1024]{0:T(1024)}, u32[]{:S(2)}) copy-start(f32[1024]{0:T(1024)} %param.12) | copy-start | bytes 12292
  111.1 5.4 %copy-start = (f32[1024]{0:T(1024)S(1)}, f32[1024]{0:T(1024)}, u32[]{:S(2)}) copy-start(f32[1024]{0:T(1024)} %param.11) | copy-start | bytes 12292
  113.9 2.4 copy-start.14
  163.6 1.3 copy-start.1
  164.9 1.3 copy-start.2
  166.2 1.4 copy-start.3
  352.5 3.2 copy-start.6
  355.7 2.3 copy-start.5
  358.1 2.3 copy-start.4
  360.4 1.4 copy-start.7
where the time goes:
time: 367 us; the launch traced here: 363 us
  Pallas kernels  218 us (59%)
  waiting for transfers between devices  77.5 us (21%)
  matrix products  30.5 us (8%)
  local copies, waits for them, and re-layouts  15.6 us (4%)
  blocking collectives  14.1 us (4%)
  starting transfers between devices  6.15 us (2%)
    pallas_call x1, Pallas kernels, after_scan(): pl.pallas_call(functools.partial(after_kernel, levels, chips, scale), in_...  185 us
    ppermute x4, waiting for transfers between devices, from_partner(): return lax.ppermute(block, axis, route)  77.5 us
    pallas_call x1, Pallas kernels, recurrences(): pl.pallas_call(functools.partial(run_kernel, devices), grid=(width // LAN...  22.6 us
    dot_general x5, matrix products, dot(): return jnp.dot(left, right, preferred_element_type=jnp.float32)  15.7 us
    unnamed x43, local copies, waits for them, and re-layouts  15.5 us
    dot_general x4, matrix products, dot_trans(): lax.dot_general(left, right, (((1,), (1,)), ((), ())), preferred_element_...  14.8 us
    all_gather x1, blocking collectives, recurrences(): totals = lax.all_gather(totals, 'seq')  14.1 us
    pallas_call x1, Pallas kernels, recurrences(): pl.pallas_call(ends_kernel, grid=(width // LANES,), in_specs=[big, big, b...  10.4 us
  transfers between devices with their start and end apart: 4, of which 3 were waited for; matrix products, arithmetic and copies ran while one was open for 6% of the time, Pallas kernels for 0%

commit v1 on v0

--- a/solution.py
+++ b/solution.py
@@ -7,20 +7,9 @@
 from jax.experimental.pallas import tpu as pltpu
 from jax.sharding import PartitionSpec as P
 
-SEGMENTS = 32
 LANES = 128
 MESH = pl.DeviceIdType.MESH
 F32, BF16 = jnp.float32, jnp.bfloat16
-
-
-def from_partner(block, axis, distance):
-    count = lax.axis_size(axis)
-    route = []
-    for low in range(count):
-        high = low | 1 << distance
-        if high != low and high < count:
-            route += [(low, high), (high, low)]
-    return lax.ppermute(block, axis, route)
 
 
 def dot(left, right):
@@ -39,128 +28,371 @@
     )
 
 
-def every(ref, step):
-    return ref[pl.ds(step, SEGMENTS, stride=ref.shape[0] // SEGMENTS), :]
-
-
-def ends_kernel(drive, out_cot, gate, keep, boosts, seg_ref, tot_ref, x_ref, g_ref):
-    lam = keep[...]
-    scale = jnp.sqrt(1.0 - lam * lam)
-    x_ref[...] = scale * drive[...].astype(jnp.float32)
-    g_ref[...] = out_cot[...] * gate[...]
-    steps = x_ref.shape[0] // SEGMENTS
-    shape = (SEGMENTS, LANES)
-    lam = jnp.broadcast_to(lam, shape)
-    state = jnp.zeros(shape, jnp.float32)
-    prod = jnp.ones(shape, jnp.float32)
-    for i in range(steps):
-        a = every(boosts, i) * lam
-        state = a * state + every(x_ref, i)
-        prod = a * prod
-    back = jnp.zeros(shape, jnp.float32)
-    for i in reversed(range(steps)):
-        a = every(boosts, i) * lam
-        back = a * (every(g_ref, i) + back)
-    seg_ref[0] = prod
-    seg_ref[1] = state
-    seg_ref[2] = back
-    p = jnp.ones((1, LANES), jnp.float32)
-    h = jnp.zeros((1, LANES), jnp.float32)
-    c = jnp.zeros((1, LANES), jnp.float32)
-    for s in range(SEGMENTS):
-        here = prod[s : s + 1]
-        h = here * h + state[s : s + 1]
-        p = here * p
-        r = SEGMENTS - 1 - s
-        c = prod[r : r + 1] * c + back[r : r + 1]
-    tot_ref[0] = p
-    tot_ref[1] = h
-    tot_ref[2] = c
-
-
-def run_kernel(
-    devices, drive, out_cot, gate, keep, boosts, seg, tots, place,
-    mixed, gate_pre, drive_grad, x_ref, g_ref, start_ref, stop_ref,
-):
-    lam = keep[...]
-    scale = jnp.sqrt(1.0 - lam * lam)
-    x_ref[...] = scale * drive[...].astype(jnp.float32)
-    g_ref[...] = out_cot[...] * gate[...]
-    steps = x_ref.shape[0] // SEGMENTS
-    shape = (SEGMENTS, LANES)
-    here = place[...]
-    h = jnp.zeros((1, LANES), jnp.float32)
-    c = jnp.zeros((1, LANES), jnp.float32)
+SEGMENT = 16
+CHUNK = SEGMENT * SEGMENT
+
+
+def swapped():
+    row = lax.broadcasted_iota(jnp.int32, (CHUNK, CHUNK), 0)
+    col = lax.broadcasted_iota(jnp.int32, (CHUNK, CHUNK), 1)
+    return (lax.rem(row, SEGMENT) * SEGMENT + lax.div(row, SEGMENT) == col).astype(BF16)
+
+
+def before_kernel(levels, devices, *refs):
+    it = iter(refs)
+    source, cotangent, entering, leaving, switch, keep, boosts = (next(it) for _ in range(7))
+    z_out = [next(it) for _ in range(levels)]
+    m_out = [next(it) for _ in range(levels)]
+    e_out = [next(it) for _ in range(levels)]
+    mixed_out, gate_out, drive_out = (next(it) for _ in range(3))
+    w_in, w_out, w_gate, zs, ms, es, shares, sent = (next(it) for _ in range(8))
+    drive, out_cot, gate, mixed, gate_pre, drive_grad = (next(it) for _ in range(6))
+    totals, prod, ends, backs, carry, order = (next(it) for _ in range(6))
+    load_sem, chunk_sem, z_send, z_recv, s_send, s_recv, t_send, t_recv, store_sem = (
+        next(it) for _ in range(9)
+    )
+    tokens, width = drive.shape
+    chunks = tokens // CHUNK
+    seq, chan = lax.axis_index("seq"), lax.axis_index("chan")
+
+    def partner(level):
+        d = 1 << level
+        bit = lax.rem(lax.div(chan, d), 2)
+        return {"chan": chan + d * (1 - 2 * bit)}
+
+    def rows(c):
+        return pl.ds(c * CHUNK, CHUNK)
+
+    def load(n, source, target):
+        return pltpu.make_async_copy(source, target, load_sem.at[n])
+
+    def weight(weights, into, level, part, n):
+        at = pl.ds(part * width, width)
+        return load(n, weights.at[level, at], into.at[level, at])
+
+    def load_z(c):
+        return pltpu.make_async_copy(source.at[rows(c)], zs.at[0, rows(c)], chunk_sem.at[c])
+
+    def load_e(c):
+        return pltpu.make_async_copy(
+            cotangent.at[rows(c)], es.at[levels - 1, rows(c)], chunk_sem.at[chunks + c]
+        )
+
+    load_w = {}
+    wanted = []
+    for step in range(levels):
+        down = levels - 1 - step
+        wanted += [("out", down, 1), ("in", step, 0), ("in", step, 1), ("out", down, 0)]
+    for n, (which, level, part) in enumerate(wanted):
+        load_w[which, level, part] = weight(
+            *((entering, w_in) if which == "in" else (leaving, w_out)), level, part, n
+        )
+    load_gate = load(4 * levels, switch, w_gate)
+    arrived = set()
+
+    def need(*key):
+        if key not in arrived:
+            arrived.add(key)
+            load_w[key].wait()
+
+    for c in reversed(range(chunks)):
+        load_e(c).start()
+        if c == chunks - 1:
+            load_w[wanted[0]].start()
+    for c in range(chunks):
+        load_z(c).start()
+    load_gate.start()
+    for key in wanted[1:]:
+        load_w[key].start()
+
+    barrier = pltpu.get_barrier_semaphore()
+    for level in range(levels):
+        pl.semaphore_signal(barrier, inc=1, device_id=partner(level), device_id_type=MESH)
+    for k in range(1, devices):
+        pl.semaphore_signal(
+            barrier, inc=1, device_id={"seq": lax.rem(seq + k, devices)}, device_id_type=MESH
+        )
+    pl.semaphore_wait(barrier, levels + devices - 1)
+
+    def remote(source, target, send, recv, device):
+        return pltpu.make_async_remote_copy(
+            src_ref=source, dst_ref=target, send_sem=send, recv_sem=recv,
+            device_id=device, device_id_type=MESH,
+        )
+
+    def send_z(level, c):
+        n = level * chunks + c
+        block = source.at[rows(c)] if level == 0 else zs.at[level, rows(c)]
+        return remote(block, ms.at[level, rows(c)], z_send.at[n], z_recv.at[n], partner(level))
+
+    def send_share(level, c):
+        n = level * chunks + c
+        return remote(
+            sent.at[level, rows(c)], shares.at[level, rows(c)],
+            s_send.at[n], s_recv.at[n], partner(level),
+        )
+
+    def send_totals(k):
+        return remote(
+            totals.at[seq], totals.at[seq], t_send.at[k - 1], t_recv.at[k - 1],
+            {"seq": lax.rem(seq + k, devices)},
+        )
+
+    def wait_totals(k):
+        there = totals.at[lax.rem(seq + devices - k, devices)]
+        remote(
+            there, there, t_send.at[k - 1], t_recv.at[k - 1],
+            {"seq": lax.rem(seq + k, devices)},
+        ).wait_recv()
+
+    for c in range(chunks):
+        send_z(0, c).start()
+    order[...] = swapped()
+
+    def in_order(ref, level, c):
+        ref[level, rows(c), :] = dot(order[...], ref[level, rows(c), :]).astype(BF16)
+
+    def share(level, c):
+        need("out", level, 1)
+        sent[level, rows(c), :] = dot_trans(
+            es[level, rows(c), :], w_out[level, pl.ds(width, width), :]
+        ).astype(BF16)
+        send_share(level, c).start()
+
+    for c in reversed(range(chunks)):
+        load_e(c).wait()
+        in_order(es, levels - 1, c)
+        share(levels - 1, c)
+    load_gate.wait()
+    for c in range(chunks):
+        load_z(c).wait()
+        in_order(zs, 0, c)
+        gate[rows(c), :] = jax.nn.sigmoid(dot(zs[0, rows(c), :], w_gate[...]))
+
+    piece = min(256, width)
+
+    def tile(c, i, lane):
+        return pl.ds(c * CHUNK + i * SEGMENT, SEGMENT), pl.ds(lane, LANES)
+
+    def for_lanes(run):
+        @pl.loop(0, width // piece)
+        def _(n):
+            run([pl.multiple_of(n * piece, piece) + q for q in range(0, piece, LANES)])
+
+    def lane_row(lane):
+        lam = keep[:, pl.ds(lane, LANES)]
+        return lam, jnp.sqrt(1.0 - lam * lam)
+
+    def wide(row):
+        return jnp.broadcast_to(row, (SEGMENT, LANES))
+
+    def ends_forward(c):
+        @for_lanes
+        def _(lanes):
+            for lane in lanes:
+                at = pl.ds(lane, LANES)
+                lam, scale = (wide(v) for v in lane_row(lane))
+                state = jnp.zeros((SEGMENT, LANES), F32)
+                p = jnp.ones((SEGMENT, LANES), F32)
+                for i in range(SEGMENT):
+                    r, at = tile(c, i, lane)
+                    a = boosts[r, :] * lam
+                    state = a * state + scale * drive[r, at].astype(F32)
+                    p = a * p
+                span = pl.ds(c * SEGMENT, SEGMENT)
+                prod[span, at] = p
+                run = carry[0:1, at]
+                grown = carry[1:2, at]
+                starts, growths = [], []
+                for s in range(SEGMENT):
+                    starts.append(run)
+                    growths.append(grown)
+                    run = p[s : s + 1] * run + state[s : s + 1]
+                    grown = p[s : s + 1] * grown
+                ends[0, span, at] = jnp.concatenate(starts, axis=0)
+                ends[1, span, at] = jnp.concatenate(growths, axis=0)
+                carry[0:1, at] = run
+                carry[1:2, at] = grown
+
+    def ends_backward(c):
+        @for_lanes
+        def _(lanes):
+            for lane in lanes:
+                at = pl.ds(lane, LANES)
+                lam = wide(lane_row(lane)[0])
+                back = jnp.zeros((SEGMENT, LANES), F32)
+                p = jnp.ones((SEGMENT, LANES), F32)
+                for i in reversed(range(SEGMENT)):
+                    r, at = tile(c, i, lane)
+                    a = boosts[r, :] * lam
+                    back = a * (out_cot[r, at] * gate[r, at] + back)
+                    p = a * p
+                span = pl.ds(c * SEGMENT, SEGMENT)
+                run = carry[2:3, at]
+                grown = carry[3:4, at]
+                starts, growths = [None] * SEGMENT, [None] * SEGMENT
+                for s in reversed(range(SEGMENT)):
+                    starts[s] = run
+                    growths[s] = grown
+                    run = p[s : s + 1] * run + back[s : s + 1]
+                    grown = p[s : s + 1] * grown
+                backs[0, span, at] = jnp.concatenate(starts, axis=0)
+                backs[1, span, at] = jnp.concatenate(growths, axis=0)
+                carry[2:3, at] = run
+                carry[3:4, at] = grown
+
+    carry[...] = jnp.zeros_like(carry)
+    carry[1:2, :] = jnp.ones((1, width), F32)
+    carry[3:4, :] = jnp.ones((1, width), F32)
+
+    stores = []
+
+    def store(ref, out):
+        copy = pltpu.make_async_copy(ref, out, store_sem.at[len(stores)])
+        copy.start()
+        stores.append(copy)
+
+    top, bot = pl.ds(0, width), pl.ds(width, width)
+    store(zs.at[0], z_out[0])
+    store(es.at[levels - 1], e_out[levels - 1])
+    for step in range(levels):
+        down = levels - 1 - step
+        for n in range(chunks):
+            c = n
+            send_z(step, c).wait_recv()
+            if step == 0:
+                in_order(ms, 0, c)
+            need("in", step, 0)
+            need("in", step, 1)
+            summed = (
+                dot(zs[step, rows(c), :], w_in[step, top, :])
+                + dot(ms[step, rows(c), :], w_in[step, bot, :])
+            ).astype(BF16)
+            if step + 1 < levels:
+                zs[step + 1, rows(c), :] = summed
+                send_z(step + 1, c).start()
+            else:
+                drive[rows(c), :] = summed
+                ends_forward(c)
+            c = chunks - 1 - n
+            send_share(down, c).wait_recv()
+            need("out", down, 0)
+            total = dot_trans(es[down, rows(c), :], w_out[down, top, :])
+            total = total + shares[down, rows(c), :].astype(F32)
+            if down > 0:
+                es[down - 1, rows(c), :] = total.astype(BF16)
+                share(down - 1, c)
+            else:
+                out_cot[rows(c), :] = total
+                ends_backward(c)
+        store(ms.at[step], m_out[step])
+        if step + 1 < levels:
+            store(zs.at[step + 1], z_out[step + 1])
+            store(es.at[down - 1], e_out[down - 1])
+
+    totals[seq, 0:1, :] = carry[1:2, :]
+    totals[seq, 1:2, :] = carry[0:1, :]
+    totals[seq, 2:3, :] = carry[2:3, :]
+    for k in range(1, devices):
+        send_totals(k).start()
+    for k in range(1, devices):
+        wait_totals(k)
+    h = jnp.zeros((1, width), F32)
+    b = jnp.zeros((1, width), F32)
     for k in range(devices):
-        h = jnp.where(k < here, tots[k, 0] * h + tots[k, 1], h)
+        h = jnp.where(k < seq, totals[k, 0:1] * h + totals[k, 1:2], h)
         r = devices - 1 - k
-        c = jnp.where(r > here, tots[r, 0] * c + tots[r, 2], c)
-    for s in range(SEGMENTS):
-        start_ref[s : s + 1] = h
-        h = seg[0, s : s + 1] * h + seg[1, s : s + 1]
-        r = SEGMENTS - 1 - s
-        stop_ref[r : r + 1] = c
-        c = seg[0, r : r + 1] * c + seg[2, r : r + 1]
-    lam = jnp.broadcast_to(lam, shape)
-    state = start_ref[...]
-    back = stop_ref[...]
-    for i in range(steps):
-        state = every(boosts, i) * lam * state + every(x_ref, i)
-        x_ref[pl.ds(i, SEGMENTS, stride=steps), :] = state
-        r = steps - 1 - i
-        total = every(g_ref, r) + back
-        g_ref[pl.ds(r, SEGMENTS, stride=steps), :] = total
-        back = every(boosts, r) * lam * total
-    sig = gate[...]
-    product = x_ref[...] * sig
-    mixed[...] = product.astype(jnp.bfloat16)
-    gate_pre[...] = (out_cot[...] * product * (1.0 - sig)).astype(jnp.bfloat16)
-    drive_grad[...] = (scale * g_ref[...]).astype(jnp.bfloat16)
-
-
-def recurrences(drive, out_cot, gate, keep, boosts):
-    tokens, width = drive.shape
+        b = jnp.where(r > seq, totals[r, 0:1] * b + totals[r, 2:3], b)
+    carry[0:1, :] = h
+    carry[2:3, :] = b
+
+    for c in range(chunks):
+        span = pl.ds(c * SEGMENT, SEGMENT)
+
+        @for_lanes
+        def _(lanes):
+            for lane in lanes:
+                at = pl.ds(lane, LANES)
+                lam, scale = (wide(v) for v in lane_row(lane))
+                state = ends[0, span, at] + ends[1, span, at] * wide(carry[0:1, at])
+                back = backs[0, span, at] + backs[1, span, at] * wide(carry[2:3, at])
+                for i in range(SEGMENT):
+                    r, at = tile(c, i, lane)
+                    state = boosts[r, :] * lam * state + scale * drive[r, at].astype(F32)
+                    sig = gate[r, at]
+                    product = state * sig
+                    mixed[r, at] = product.astype(BF16)
+                    gate_pre[r, at] = (out_cot[r, at] * product * (1.0 - sig)).astype(BF16)
+                for i in reversed(range(SEGMENT)):
+                    r, at = tile(c, i, lane)
+                    total = out_cot[r, at] * gate[r, at] + back
+                    drive_grad[r, at] = (scale * total).astype(BF16)
+                    back = boosts[r, :] * lam * total
+
+    store(mixed, mixed_out)
+    store(gate_pre, gate_out)
+    store(drive_grad, drive_out)
+    for copy in stores:
+        copy.wait()
+    for level in range(levels):
+        for c in range(chunks):
+            send_z(level, c).wait_send()
+            send_share(level, c).wait_send()
+    for k in range(1, devices):
+        send_totals(k).wait_send()
+
+
+def before_scan(source, cotangent, entering, leaving, switch, keep, boosts):
+    levels = entering.shape[0]
+    tokens, width = source.shape
     devices = lax.axis_size("seq")
-    keep = keep[None, :]
-    boosts = jnp.broadcast_to(boosts[:, None], (tokens, LANES))
-    big = pl.BlockSpec((tokens, LANES), lambda j: (0, j))
-    row = pl.BlockSpec((1, LANES), lambda j: (0, j))
-    same = pl.BlockSpec((tokens, LANES), lambda j: (0, 0))
-    seg_spec = pl.BlockSpec((3, SEGMENTS, LANES), lambda j: (0, 0, j))
-    scratch = pltpu.VMEM((tokens, LANES), jnp.float32)
-    small = pltpu.VMEM((SEGMENTS, LANES), jnp.float32)
-    area = tokens * width
-    seg, totals = pl.pallas_call(
-        ends_kernel,
-        grid=(width // LANES,),
-        in_specs=[big, big, big, row, same],
-        out_specs=[seg_spec, pl.BlockSpec((3, 1, LANES), lambda j: (0, 0, j))],
-        out_shape=[
-            jax.ShapeDtypeStruct((3, SEGMENTS, width), jnp.float32),
-            jax.ShapeDtypeStruct((3, 1, width), jnp.float32),
+    chunks = tokens // CHUNK
+    boosts = boosts.reshape(chunks, SEGMENT, SEGMENT).swapaxes(1, 2).reshape(tokens, 1)
+    boosts = jnp.broadcast_to(boosts, (tokens, LANES))
+    hbm = pl.BlockSpec(memory_space=pl.ANY)
+    vmem = pl.BlockSpec(memory_space=pltpu.VMEM)
+    dma = pltpu.SemaphoreType.DMA
+    block = jax.ShapeDtypeStruct((tokens, width), BF16)
+    count = 3 * levels + 3
+    segments = tokens // SEGMENT
+    result = pl.pallas_call(
+        functools.partial(before_kernel, levels, devices),
+        in_specs=[hbm] * 5 + [vmem] * 2,
+        out_specs=[hbm] * count,
+        out_shape=[block] * count,
+        scratch_shapes=[
+            pltpu.VMEM((levels, 2 * width, width), BF16),
+            pltpu.VMEM((levels, 2 * width, width), BF16),
+            pltpu.VMEM((width, width), BF16),
+            *[pltpu.VMEM((levels, tokens, width), BF16)] * 5,
+            pltpu.VMEM((tokens, width), BF16),
+            pltpu.VMEM((tokens, width), F32),
+            pltpu.VMEM((tokens, width), F32),
+            *[pltpu.VMEM((tokens, width), BF16)] * 3,
+            pltpu.VMEM((devices, 8, width), F32),
+            pltpu.VMEM((segments, width), F32),
+            pltpu.VMEM((2, segments, width), F32),
+            pltpu.VMEM((2, segments, width), F32),
+            pltpu.VMEM((8, width), F32),
+            pltpu.VMEM((CHUNK, CHUNK), BF16),
+            dma((4 * levels + 1,)), dma((2 * chunks,)),
+            *[dma((levels * chunks,))] * 4,
+            *[dma((devices - 1,))] * 2,
+            dma((count,)),
         ],
-        scratch_shapes=[scratch, scratch],
-        compiler_params=pltpu.CompilerParams(vmem_limit_bytes=24 << 20),
-        cost_estimate=pl.CostEstimate(flops=10 * area, bytes_accessed=10 * area, transcendentals=0),
-        name="ends",
-    )(drive, out_cot, gate, keep, boosts)
-    totals = lax.all_gather(totals, "seq")
-    place = jnp.full((1, LANES), lax.axis_index("seq"), jnp.int32)
-    return pl.pallas_call(
-        functools.partial(run_kernel, devices),
-        grid=(width // LANES,),
-        in_specs=[
-            big, big, big, row, same, seg_spec,
-            pl.BlockSpec((devices, 3, 1, LANES), lambda j: (0, 0, 0, j)),
-            pl.BlockSpec((1, LANES), lambda j: (0, 0)),
-        ],
-        out_specs=[big, big, big],
-        out_shape=[jax.ShapeDtypeStruct((tokens, width), jnp.bfloat16)] * 3,
-        scratch_shapes=[scratch, scratch, small, small],
-        compiler_params=pltpu.CompilerParams(vmem_limit_bytes=24 << 20),
-        cost_estimate=pl.CostEstimate(flops=20 * area, bytes_accessed=16 * area, transcendentals=0),
-        name="recurrences",
-    )(drive, out_cot, gate, keep, boosts, seg, totals, place)
+        compiler_params=pltpu.CompilerParams(
+            collective_id=1, has_side_effects=True, vmem_limit_bytes=60 << 20
+        ),
+        cost_estimate=pl.CostEstimate(
+            flops=2 * tokens * width * width * (4 * levels + 1),
+            bytes_accessed=60 * tokens * width, transcendentals=tokens * width,
+        ),
+        name="before_scan",
+    )(source, cotangent, entering, leaving, switch, keep[None, :], boosts)
+    return (
+        result[:levels], result[levels : 2 * levels], result[2 * levels : 3 * levels],
+        *result[3 * levels :],
+    )
 
 
 SLOTS = 4
@@ -175,7 +407,7 @@
     mixed, gate_pre, drive_grad, entering, leaving, switch = (next(it) for _ in range(6))
     layer_out, token_grads, in_grads, out_grads, gate_grads = (next(it) for _ in range(5))
     stage, part, sums, gate_sums, right, left, gate_right, gate_left = (next(it) for _ in range(8))
-    mates, shares, outs, cots, sent, final = (next(it) for _ in range(6))
+    mates, shares, outs, cots, sent, final, order = (next(it) for _ in range(7))
     load_sem, sib_send, sib_recv, right_send, right_recv, left_send, left_recv = (
         next(it) for _ in range(7)
     )
@@ -373,7 +605,7 @@
             ).astype(BF16)
 
     work = []
-    tall = min(256, tokens)
+    tall = CHUNK
 
     def tiles(store):
         @pl.loop(0, tokens // tall)
@@ -485,7 +717,8 @@
             def store(at):
                 total = dot(held[at, :], bufs[0][...]) + dot(mate[at, :], bufs[1][...])
                 if last:
-                    mates[0, at, :] = (bufs[-1][at, :].astype(F32) + total).astype(BF16)
+                    total = (bufs[-1][at, :].astype(F32) + total).astype(BF16)
+                    mates[0, at, :] = dot(order[...], total).astype(BF16)
                 else:
                     outs[step, at, :] = total.astype(BF16)
 
@@ -516,7 +749,7 @@
                 if last:
                     total = total + dot_trans(bufs[-3][at, :], bufs[-2][...])
                     total = total + bufs[-1][at, :].astype(F32)
-                    shares[0, at, :] = total.astype(BF16)
+                    shares[0, at, :] = dot(order[...], total.astype(BF16)).astype(BF16)
                 else:
                     cots[step, at, :] = total.astype(BF16)
 
@@ -529,6 +762,7 @@
         task(loads, run)
 
     swap_out(0, mixed).start()
+    order[...] = swapped()
     share_task(0)
     grad_task(0, 0, hbm(z[0]), hbm(gate_pre), True)
     for step in range(levels):
@@ -623,6 +857,7 @@
             pltpu.VMEM((levels - 1, tokens, width), BF16),
             pltpu.VMEM((tokens, width), BF16),
             pltpu.VMEM((2, rows, width), F32),
+            pltpu.VMEM((CHUNK, CHUNK), BF16),
             dma((SLOTS,)), dma((blocks,)), dma((blocks,)),
             dma((hops,)), dma((hops,)), dma((hops,)), dma((hops,)),
             dma((2 * levels,)), dma((2 * levels,)), dma((2,)), dma((2,)),
@@ -637,15 +872,6 @@
     )(*args)
 
 
-def share_of(cotangent, weight):
-    return dot_trans(cotangent, weight[cotangent.shape[1] :]).astype(jnp.bfloat16)
-
-
-def transposed_step(cotangent, weight, received):
-    width = cotangent.shape[1]
-    return dot_trans(cotangent, weight[:width]) + received.astype(jnp.float32)
-
-
 def shards(
     layer_source,
     entering,
@@ -655,29 +881,13 @@
     position_boosts,
     result_cotangent,
 ):
-    levels = entering.shape[0]
-    width = layer_source.shape[1]
     scale = float(layer_source.shape[0] * lax.axis_size("seq")) ** (-0.5)
-
-    z, z_mates = [layer_source], []
-    e = [None] * levels + [result_cotangent]
-    for step in range(levels):
-        z_mates.append(from_partner(z[step], "chan", step))
-        down = levels - 1 - step
-        share = from_partner(share_of(e[down + 1], leaving[down]), "chan", down)
-        e[down] = transposed_step(e[down + 1], leaving[down], share)
-        if down > 0:
-            e[down] = e[down].astype(jnp.bfloat16)
-        summed = dot(z[step], entering[step, :width]) + dot(z_mates[step], entering[step, width:])
-        z.append(summed.astype(jnp.bfloat16))
-    gate = jax.nn.sigmoid(dot(layer_source, switch))
-
-    mixed, gate_pre_grad, drive_grad = recurrences(
-        z[levels], e[0], gate, channel_persistence, position_boosts
+    z, z_mates, e, mixed, gate_pre_grad, drive_grad = before_scan(
+        layer_source, result_cotangent, entering, leaving, switch,
+        channel_persistence, position_boosts,
     )
     return after_scan(
-        z[:levels], z_mates, e[1:], mixed, gate_pre_grad, drive_grad,
-        entering, leaving, switch, scale,
+        z, z_mates, e, mixed, gate_pre_grad, drive_grad, entering, leaving, switch, scale
     )
 
 

time: 367 us -> 314 us (0.86)
  waiting for transfers between devices: 77.5 us -> 0 us
  Pallas kernels: 218 us -> 295 us
  matrix products: 30.5 us -> 0 us
  blocking collectives: 14.1 us -> 0 us
  starting transfers between devices: 6.15 us -> 0 us
    pallas_call x2 -> x1, Pallas kernels: 32.9 us -> 114 us  [before_scan(): pl.pallas_call(functools.partial(before_kernel, levels, devices), in_spec...]
    ppermute x4 -> x0, waiting for transfers between devices: 77.5 us -> none  [from_partner(): return lax.ppermute(block, axis, route)]
    dot_general x9 -> x0, matrix products: 30.5 us -> none  [the longest x5 15.7 us: dot(): return jnp.dot(left, right, preferred_element_type=jnp.float32)]
    all_gather x1 -> x0, blocking collectives: 14.1 us -> none  [recurrences(): totals = lax.all_gather(totals, 'seq')]
    ppermute x4 -> x0, starting transfers between devices: 6.15 us -> none  [from_partner(): return lax.ppermute(block, axis, route)]
    unnamed x43 -> x13, local copies, waits for them, and re-layouts: 15.5 us -> 10.1 us
  transfers between devices with their start and end apart: 4 -> 0, of which waited for: 3 -> 0; matrix products, arithmetic and copies ran while one was open for 6% -> 0% of each run, Pallas kernels for 0% -> 0%
where the time goes in v1:
time: 314 us; the launch traced here: 308 us
  Pallas kernels  295 us (94%)
  local copies, waits for them, and re-layouts  12 us (4%)
    pallas_call x1, Pallas kernels, after_scan(): pl.pallas_call(functools.partial(after_kernel, levels, chips, scale), in_...  181 us
    pallas_call x1, Pallas kernels, before_scan(): pl.pallas_call(functools.partial(before_kernel, levels, devices), in_spec...  114 us
    unnamed x13, local copies, waits for them, and re-layouts  10.1 us

profile of v1, /device:TPU:8, one launch (start us, length us, event | category | flops | bytes accessed | tf_op | source)
XLA Modules:
  0.0 308.3 jit_solution(7757826037455619530)
XLA Ops:
  0.6 0.8 reshape.15
  1.4 0.1 copy.12
  1.5 0.1 broadcast_in_dim.11
  1.5 1.0 broadcast_in_dim.12.refs_6_
  2.5 114.1 %before_scan.1 = (bf16[1024,1024]{1,0:T(8,128)(2,1)}, bf16[1024,1024]{1,0:T(8,128)(2,1)}, bf16[1024,1024]{1,0:T(8,128)(2,1)}, bf16[1024,1024]{1,0:T(8,128)(2,1)}...) custom-call(bf16[1024,1024]{1,0:T(8,128)(2,1)} %refs_0_.1, ...), custom_call_target="tpu_custom_call" | custom-call | flops 19327352832 | bytes 62914560 | tf_op jit(solution)/shard_map/before_scan/pallas_call | solution.py:358
  116.7 181.3 %after_scan.1 = (bf16[1024,1024]{1,0:T(8,128)(2,1)}, bf16[1024,1024]{1,0:T(8,128)(2,1)}, f32[2,256,1024]{2,1,0:T(8,128)}, f32[2,256,1024]{2,1,0:T(8,128)}, f32[128,1024]{1,0:T(8,128)}) custom-call(bf16[1024,1024]{1,0:T(8,128)(2,1)} %get-tuple-element.14.refs_0_, bf16[1024,1024]{1,0:T(8,128)(2,1)} %get-tuple-element.15.refs_1_, ...), custom_call_target="tpu_custom_call" | custom-call | flops 38654705664 | bytes 62914560 | tf_op jit(solution)/shard_map/after_scan/pallas_call | solution.py:834
  297.9 0.0 copy-start.2
  297.9 3.2 %copy.18 = bf16[1024,1024]{1,0:T(8,128)(2,1)} copy(bf16[1024,1024]{1,0:T(8,128)(2,1)} %get-tuple-element.28) | data formatting | bytes 4194304
  301.2 0.0 copy-done.2
  301.2 0.0 copy-start.1
  301.2 1.3 copy.19
  302.5 1.0 copy-done.1
  303.5 0.0 copy-start
  303.5 1.3 copy.20
  304.8 1.0 copy-done
  305.9 0.0 copy-start.3
  305.9 1.3 copy.21
  307.2 0.1 copy-done.3
  307.3 0.8 copy.22
Async XLA Ops:
  297.9 3.2 %copy-start.2 = (bf16[1024,1024]{1,0:T(8,128)(2,1)S(1)}, bf16[1024,1024]{1,0:T(8,128)(2,1)}, u32[]{:S(2)}) copy-start(bf16[1024,1024]{1,0:T(8,128)(2,1)} %get-tuple-element.29) | copy-start | bytes 6291460
  301.2 2.3 copy-start.1
  303.5 2.3 copy-start
  305.9 1.4 copy-start.3
